TPU v7x, 128 devices: a whole 4x4x4 slice. The times are simulated.
128 devices in a mesh: dp: 8 (over y, core), tensor: 16 (over z, x).
Axes of the slice: x: 4, y: 4, z: 4, core: 2. Of those that a mesh axis runs over, the one named last changes fastest.
Arguments:
- hidden: bfloat16 [4096, 1536], P(('dp', 'tensor')), may hold values from -6 to 6
- norm_gain: float32 [1536], replicated, may hold values from 0.25 to 1.75
- unembed: bfloat16 [1536, 77824], P(None, 'tensor'), may hold values from -0.15625 to 0.15625
- verifier_logits: bfloat16 [4096, 77824], P('dp', 'tensor'), may hold values from -4 to 340
- served_ids: int32 [4096], P('dp'), may hold values from 0 to 77823
- accepted: int32 [512], P('dp'), may hold values from 0 to 8
Outputs:
- grad_unembed: bfloat16 [1536, 77824], P('dp', 'tensor')
- grad_hidden: bfloat16 [4096, 1536], P(('dp', 'tensor'))
All inputs are finite; a program needn't handle non-finite values.
Results may differ from a plain program's by a relative error of at most 0.02.
Values may be sent and summed in bfloat16 or wider, within the bound.
A program may use at most 128 MiB of HBM per device.

v0:
```python
import jax
import jax.numpy as jnp
from jax import lax
from jax.sharding import PartitionSpec as P

DRAFT = 8


def totals(logits):
    top = jnp.max(logits, axis=-1)
    return (top, jnp.sum(jnp.exp(logits - top[:, None]), axis=-1))


def logit_grads(drafter, verif, row_ids, weights, stats):
    verif_max, verif_sum, draft_max, draft_sum = stats
    draft_prob = jnp.exp(drafter.astype(jnp.float32) - draft_max[:, None]) / draft_sum[:, None]
    verif_prob = jnp.exp(verif.astype(jnp.float32) - verif_max[:, None]) / verif_sum[:, None]
    columns = jnp.arange(drafter.shape[1], dtype=jnp.int32)[None, :]
    onehot = (row_ids[:, None] == columns).astype(jnp.float32)
    target = 0.8 * verif_prob + 0.2 * onehot
    return (weights[:, None] * (draft_prob - target)).astype(jnp.bfloat16)


def body(hidden, norm_gain, unembed, verifier_logits, served_ids, accepted):
    group_hidden = lax.all_gather(hidden, "tensor", axis=0, tiled=True)
    hid_rows = group_hidden.astype(jnp.float32)
    inverse = lax.rsqrt(jnp.mean(hid_rows * hid_rows, axis=-1, keepdims=True) + 1e-06)
    normed = hid_rows * inverse
    scaled = (normed * norm_gain).astype(jnp.bfloat16)
    drafter = jnp.dot(scaled, unembed, preferred_element_type=jnp.float32).astype(jnp.bfloat16)
    group_rows = drafter.shape[0]
    owned = hidden.shape[0]
    tensor_index = lax.axis_index("tensor")
    slot_index = jnp.arange(group_rows, dtype=jnp.int32) % DRAFT
    block_accept = jnp.repeat(accepted, DRAFT)
    row_weight = jnp.where(slot_index <= block_accept, 1.0, 0.2).astype(jnp.float32)
    owner_draft, owner_verif = (
        lax.all_to_all(drafter, "tensor", split_axis=0, concat_axis=1, tiled=True),
        lax.all_to_all(verifier_logits, "tensor", split_axis=0, concat_axis=1, tiled=True),
    )
    start = tensor_index * owned
    row_ids = lax.dynamic_slice_in_dim(served_ids, start, owned, 0)
    weights = lax.dynamic_slice_in_dim(row_weight, start, owned, 0)
    verif_max, verif_sum = totals(owner_verif.astype(jnp.float32))
    draft_max, draft_sum = totals(owner_draft.astype(jnp.float32))
    owner_grads = logit_grads(
        owner_draft, owner_verif, row_ids, weights, (verif_max, verif_sum, draft_max, draft_sum)
    )
    grad_logits = lax.all_to_all(owner_grads, "tensor", split_axis=1, concat_axis=0, tiled=True)
    grad_normed = lax.psum_scatter(
        lax.dot_general(
            grad_logits, unembed, (((1,), (1,)), ((), ())), preferred_element_type=jnp.float32
        ).astype(jnp.bfloat16),
        "tensor",
        scatter_dimension=0,
        tiled=True,
    ).astype(jnp.float32)
    own_hidden = hidden.astype(jnp.float32)
    own_inverse = lax.rsqrt(jnp.mean(own_hidden * own_hidden, axis=-1, keepdims=True) + 1e-06)
    own_normed = own_hidden * own_inverse
    grad_y = grad_normed * norm_gain
    inner = jnp.mean(grad_y * own_normed, axis=-1, keepdims=True)
    grad_hidden = (own_inverse * (grad_y - own_normed * inner)).astype(jnp.bfloat16)
    grad_unembed = lax.psum_scatter(
        lax.dot_general(
            scaled, grad_logits, (((0,), (0,)), ((), ())), preferred_element_type=jnp.float32
        ).astype(jnp.bfloat16),
        "dp",
        scatter_dimension=0,
        tiled=True,
    )
    return (grad_unembed, grad_hidden)


def solution(mesh):
    return jax.shard_map(
        body,
        mesh=mesh,
        in_specs=(
            P(("dp", "tensor"), None),
            P(),
            P(None, "tensor"),
            P("dp", "tensor"),
            P("dp"),
            P("dp"),
        ),
        out_specs=(P("dp", "tensor"), P(("dp", "tensor"), None)),
        check_vma=False,
    )
```

profile of v0, /device:TPU:1, one launch (start us, length us, event | category | flops | bytes accessed | tf_op | source)
XLA Modules:
  0.0 451.1 jit_solution(6782832633157493997)
XLA Ops:
  7.2 0.7 all-gather.2.cloned.1.call-update
  7.9 8.5 %all-to-all-start.1 = ((bf16[16,32,4864]{2,1,0:T(8,128)(2,1)}), bf16[16,32,4864]{2,1,0:T(8,128)(2,1)}, u32[]{:S(2)}, u32[]{:S(2)}) async-start(bf16[16,32,4864]{2,1,0:T(8,128)(2,1)} %bitcast.19), calls=%async_computation.1 | async-start | bytes 9961472 | tf_op jit(solution)/shard_map/all_to_all | solution.py:39
  16.4 84.3 %all-gather.2.cloned.1.call-done = bf16[512,1536]{1,0:T(8,128)(2,1)} async-done(((bf16[32,1536]{1,0:T(8,128)(2,1)}), bf16[512,1536]{1,0:T(8,128)(2,1)}) %all-gather.2.cloned.1.call-update) | async-done | bytes 1572880 | tf_op jit(solution)/shard_map/all_gather | solution.py:25
  100.7 1.8 fusion.5
  102.5 15.3 %convolution_convert_fusion.1 = bf16[512,4864]{1,0:T(8,128)(2,1)} fusion(bf16[1536,4864]{1,0:T(8,128)(2,1)} %param.8, bf16[512,1536]{1,0:T(8,128)(2,1)} %all-gather.2.cloned.1.call-done, f32[1536]{0:T(1024)S(1)} %copy-done.3, f32[512]{0:T(512)S(1)} %add_rsqrt_fusion), kind=kOutput, calls=%fused_computation.9 | convolution fusion | flops 7656046592 | bytes 21504000 | tf_op jit(solution)/shard_map/dot_general | solution.py:30
  117.8 4.7 %all-to-all-start = ((bf16[16,32,4864]{2,1,0:T(8,128)(2,1)}), bf16[16,32,4864]{2,1,0:T(8,128)(2,1)}, u32[]{:S(2)}, u32[]{:S(2)}) async-start(bf16[16,32,4864]{2,1,0:T(8,128)(2,1)} %bitcast.20), calls=%async_computation | async-start | bytes 9961472 | tf_op jit(solution)/shard_map/all_to_all | solution.py:38
  122.7 0.1 reshape.96
  122.8 0.8 dynamic_slice.7
  123.7 3.2 reduce_max.30
  126.8 4.2 fusion.3
  131.0 62.6 %all-to-all-done = bf16[16,32,4864]{2,1,0:T(8,128)(2,1)} async-done(((bf16[16,32,4864]{2,1,0:T(8,128)(2,1)}), bf16[16,32,4864]{2,1,0:T(8,128)(2,1)}, u32[]{:S(2)}, u32[]{:S(2)}) %all-to-all-start) | async-done | bytes 4980768 | tf_op jit(solution)/shard_map/all_to_all | solution.py:38
  193.7 3.2 reduce_max.28
  196.8 4.2 fusion.4
  201.0 7.7 %fusion.2 = bf16[32,16,4864]{2,0,1:T(8,128)(2,1)S(1)} fusion(bf16[16,32,4864]{2,1,0:T(8,128)(2,1)} %all-to-all-done.1, bf16[16,32,4864]{2,1,0:T(8,128)(2,1)} %all-to-all-done, s32[16,4864]{1,0:T(8,128)S(1)} %multiply_add_fusion, f32[32]{0:T(128)S(1)} %fusion.3, f32[32]{0:T(128)S(1)} %reduce_max.31, f32[32]{0:T(128)S(1)} %fusion.4, f32[32]{0:T(128)S(1)} %reduce_max.29, ...), kind=kLoop, calls=%fused_computation.4 | loop fusion | flops 32374784 | bytes 15254272 | tf_op jit(solution)/shard_map/convert_element_type | solution.py:21
  208.8 61.5 %all_to_all.42 = bf16[32,16,4864]{2,0,1:T(8,128)(2,1)S(1)} all-to-all(bf16[32,16,4864]{2,0,1:T(8,128)(2,1)S(1)} %fusion.2), channel_id=1, replica_groups=mesh['dp'=8,'tensor'=16] {'tensor'}, dimensions={1} | all-to-all | bytes 9961472 | tf_op jit(solution)/shard_map/all_to_all | solution.py:49
  270.2 2.2 copy-done
  272.5 12.3 %convolution_convert_fusion.2 = bf16[512,1536]{1,0:T(8,128)(2,1)} fusion(bf16[512,4864]{1,0:T(8,128)(2,1)S(1)} %bitcast.21, bf16[1536,4864]{1,0:T(8,128)(2,1)} %param.8), kind=kOutput, calls=%fused_computation.15 | convolution fusion | flops 7651196928 | bytes 21495808 | tf_op jit(solution)/shard_map/dot_general | solution.py:51
  284.8 13.4 %convolution_convert_fusion = bf16[1536,4864]{1,0:T(8,128)(2,1)} fusion(bf16[512,4864]{1,0:T(8,128)(2,1)} %bitcast.22, bf16[512,1536]{1,0:T(8,128)(2,1)S(1)} %copy-done.1, f32[1536]{0:T(1024)S(1)} %copy-done.3, f32[512]{0:T(512)S(1)} %add_rsqrt_fusion), kind=kOutput, calls=%fused_computation | convolution fusion | flops 7661027328 | bytes 21504000 | tf_op jit(solution)/shard_map/dot_general | solution.py:65
  298.2 0.9 copy-done.2
  299.1 0.1 fusion.16
  299.2 58.4 %reduce-scatter.5.cloned.1.call-done = bf16[32,1536]{1,0:T(8,128)(2,1)} async-done(((bf16[512,1536]{1,0:T(8,128)(2,1)}), bf16[32,1536]{1,0:T(8,128)(2,1)}) %reduce-scatter.5.cloned.1.call-update) | async-done | bytes 98320 | tf_op jit(solution)/shard_map/reduce_scatter | solution.py:50
  357.6 1.1 fusion.12
  358.7 1.6 fusion.15
  360.4 84.2 %reduce-scatter.3.cloned.1.call-done = bf16[192,4864]{1,0:T(8,128)(2,1)} async-done(((bf16[1536,4864]{1,0:T(8,128)(2,1)}), bf16[192,4864]{1,0:T(8,128)(2,1)}) %reduce-scatter.3.cloned.1.call-update) | async-done | bytes 1867792 | tf_op jit(solution)/shard_map/reduce_scatter | solution.py:64
  (23 shorter events, 0.4 us)
Async XLA Ops:
  7.2 93.5 %all-gather.2.cloned.1.call-start = ((), (), s32[]{:S(2)}) async-start(), calls=%async_computation.5 | async-start | bytes 1671168 | tf_op jit(solution)/shard_map/all_gather | solution.py:25
  7.9 94.6 %copy-start.3 = (f32[1536]{0:T(1024)S(1)}, f32[1536]{0:T(1024)}, u32[]{:S(2)}) copy-start(f32[1536]{0:T(1024)} %param.7) | copy-start | bytes 18436
  7.9 109.9 %all-to-all-start.1 = ((bf16[16,32,4864]{2,1,0:T(8,128)(2,1)}), bf16[16,32,4864]{2,1,0:T(8,128)(2,1)}, u32[]{:S(2)}, u32[]{:S(2)}) async-start(bf16[16,32,4864]{2,1,0:T(8,128)(2,1)} %bitcast.19), calls=%async_computation.1 | async-start | bytes 9961472 | tf_op jit(solution)/shard_map/all_to_all | solution.py:39
  117.8 4.8 %copy-start.4 = (s32[64]{0:T(128)S(1)}, s32[64]{0:T(128)}, u32[]{:S(2)}) copy-start(s32[64]{0:T(128)} %param.11) | copy-start | bytes 772
  117.8 75.8 %all-to-all-start = ((bf16[16,32,4864]{2,1,0:T(8,128)(2,1)}), bf16[16,32,4864]{2,1,0:T(8,128)(2,1)}, u32[]{:S(2)}, u32[]{:S(2)}) async-start(bf16[16,32,4864]{2,1,0:T(8,128)(2,1)} %bitcast.20), calls=%async_computation | async-start | bytes 9961472 | tf_op jit(solution)/shard_map/all_to_all | solution.py:38
  122.6 235.0 %reduce-scatter.5.cloned.1.call-start = ((), (), s32[]{:S(2)}) async-start(), calls=%async_computation.7 | async-start | bytes 1671168 | tf_op jit(solution)/shard_map/reduce_scatter | solution.py:50
  270.2 2.2 copy-start
  272.5 12.3 %copy-start.1 = (bf16[512,1536]{1,0:T(8,128)(2,1)S(1)}, bf16[512,1536]{1,0:T(8,128)(2,1)}, u32[]{:S(2)}) copy-start(bf16[512,1536]{1,0:T(8,128)(2,1)} %all-gather.2.cloned.1.call-done) | copy-start | bytes 4718596
  284.7 159.8 %reduce-scatter.3.cloned.1.call-start = ((), (), s32[]{:S(2)}) async-start(), calls=%async_computation.6 | async-start | bytes 16809984 | tf_op jit(solution)/shard_map/reduce_scatter | solution.py:64
  298.2 0.9 copy-start.2
Sparse Core Ops, SparseCore 0:
  10.1 90.5 all-gather.1
  284.9 72.6 reduce-scatter.4
  360.6 83.8 reduce-scatter.2
where the time goes:
time: 452 us; the launch traced here: 451 us
  waiting for transfers between devices  290 us (64%)
  blocking collectives  61.5 us (14%)
  matrix products  41 us (9%)
  other arithmetic  27.2 us (6%)
  between operations  13.8 us (3%)
  starting transfers between devices  13.3 us (3%)
    all_gather x1, waiting for transfers between devices, body(): group_hidden = lax.all_gather(hidden, 'tensor', axis=0, tiled=True)  84.3 us
    reduce_scatter x1, waiting for transfers between devices, body(): lax.psum_scatter(lax.dot_general(scaled, grad_logits, (((0,), (0,)), ((),...  84.2 us
    all_to_all x1, waiting for transfers between devices, body(): lax.all_to_all(drafter, 'tensor', split_axis=0, concat_axis=1, tiled=True)  62.6 us
    all_to_all x1, blocking collectives, body(): lax.all_to_all(owner_grads, 'tensor', split_axis=1, concat_axis=0, tiled=...  61.5 us
    reduce_scatter x1, waiting for transfers between devices, body(): lax.psum_scatter(lax.dot_general(grad_logits, unembed, (((1,), (1,)), (()...  58.4 us
    dot_general x1, matrix products, body(): jnp.dot(scaled, unembed, preferred_element_type=jnp.float32)  15.3 us
    dot_general x1, matrix products, body(): lax.dot_general(scaled, grad_logits, (((0,), (0,)), ((), ())), preferred_...  13.4 us
    dot_general x1, matrix products, body(): lax.dot_general(grad_logits, unembed, (((1,), (1,)), ((), ())), preferred...  12.3 us
  transfers between devices with their start and end apart: 5, of which 4 were waited for; matrix products, arithmetic and copies ran while one was open for 9% of the time, Pallas kernels for 0%

commit v1 on v0

v1 whole, which is shorter than its diff:
```python
import functools

import jax
import jax.numpy as jnp
from jax import lax
from jax.experimental import pallas as pl
from jax.experimental.pallas import tpu as pltpu
from jax.sharding import PartitionSpec as P

DRAFT = 8
MESH = pl.DeviceIdType.MESH
F32 = jnp.float32
BF16 = jnp.bfloat16
LANES = 128
CHUNK = 256


def wait_bytes(ref, sem):
    pltpu.make_async_copy(ref, ref, sem).wait()


def to_columns(row):
    return jnp.transpose(jnp.broadcast_to(row, (LANES, LANES)))


def log_sum_rows(ref, rows, lse_ref):
    block, width = 64, ref.shape[1]

    @pl.loop(0, rows // block)
    def _(index):
        at = pl.ds(pl.multiple_of(index * block, block), block)
        tops = [ref[at, j * LANES:(j + 1) * LANES].astype(F32) for j in range(4)]
        for j in range(4, width // LANES):
            tops[j % 4] = jnp.maximum(tops[j % 4], ref[at, j * LANES:(j + 1) * LANES].astype(F32))
        top = jnp.maximum(jnp.maximum(tops[0], tops[1]), jnp.maximum(tops[2], tops[3]))
        top = jnp.max(top, axis=-1, keepdims=True)
        wide = jnp.broadcast_to(top, (block, LANES))
        sums = [jnp.zeros((block, LANES), F32) for _ in range(2)]
        for j in range(width // LANES):
            sums[j % 2] += jnp.exp(ref[at, j * LANES:(j + 1) * LANES].astype(F32) - wide)
        total = jnp.sum(sums[0] + sums[1], axis=-1, keepdims=True)
        lse_ref[at, :] = jnp.broadcast_to(top + jnp.log(total), (block, LANES))


def pack_rows(lse_ref, stat_ref, rows):
    same = lax.broadcasted_iota(jnp.int32, (LANES, LANES), 0) == lax.broadcasted_iota(jnp.int32, (LANES, LANES), 1)
    for b in range(rows // LANES):
        picked = jnp.where(same, lse_ref[b * LANES:(b + 1) * LANES, :], 0.0)
        stat_ref[0, b:b + 1, :] = jnp.sum(picked, axis=0, keepdims=True)


def combine(stat_ref):
    stats = stat_ref[...]
    top = jnp.max(stats, axis=0)
    return top + jnp.log(jnp.sum(jnp.exp(stats - top[None]), axis=0))


def kernel(n_dp, n_t, hid_ref, gain_ref, u_hbm, v_hbm, ids_ref, lw_ref, out_u, out_h,
           u_ref, v_ref, g_ref, gp_ref, sc_ref, tr_ref, ot_ref, pt_ref, p_ref, f_ref, o_ref, s_ref,
           gn_ref, gr_ref, lse_ref, a_ref, b_ref, i_ref, w_ref, vst_ref, dst_ref,
           v_sem, u_sem, ag_send, ag_recv, vs_send, vs_recv, ds_send, ds_recv, pt_send, pt_recv,
           g_send, g_recv, y_send, f_recv, o_recv, s_recv, n_send, n_recv):
    rows, width = v_ref.shape
    owned, depth = hid_ref.shape
    chunks = width // CHUNK
    part = out_u.shape[0]
    n_y = n_dp // 2
    dp, t = lax.axis_index("dp"), lax.axis_index("tensor")
    y, core = dp // 2, lax.rem(dp, 2)
    partner = (dp + 1 - 2 * core, t)
    up = (lax.rem(dp + 2, n_dp), t)
    down = (lax.rem(dp + n_dp - 2, n_dp), t)

    v_copy = pltpu.make_async_copy(v_hbm, v_ref, v_sem)
    v_copy.start()

    def columns(i):
        return pl.ds(pl.multiple_of(i * CHUNK, CHUNK), CHUNK)

    def u_copy(i):
        return pltpu.make_async_copy(u_hbm.at[:, columns(i)], u_ref.at[:, columns(i)], u_sem.at[i])

    @pl.loop(0, chunks)
    def _(i):
        u_copy(i).start()

    barrier = pltpu.get_barrier_semaphore()

    @pl.loop(1, n_t)
    def _(k):
        pl.semaphore_signal(barrier, inc=1, device_id=(dp, lax.rem(t + k, n_t)), device_id_type=MESH)

    for other in (partner, up, down):
        pl.semaphore_signal(barrier, inc=1, device_id=other, device_id_type=MESH)

    hidden = hid_ref[...].astype(F32)
    inverse = lax.rsqrt(jnp.mean(hidden * hidden, axis=-1, keepdims=True) + 1e-06)
    own = pl.ds(pl.multiple_of(t * owned, owned), owned)
    sc_ref[own, :] = (hidden * inverse * gain_ref[...]).astype(BF16)
    pl.semaphore_wait(barrier, n_t + 2)

    @pl.loop(1, n_t)
    def _(k):
        pltpu.make_async_remote_copy(
            sc_ref.at[own], sc_ref.at[own], ag_send, ag_recv,
            device_id=(dp, lax.rem(t + k, n_t)), device_id_type=MESH).start()

    v_copy.wait()
    log_sum_rows(v_ref, rows, lse_ref)
    vst_ref[0] = jnp.zeros(vst_ref.shape[1:], F32)
    dst_ref[0] = jnp.zeros(dst_ref.shape[1:], F32)
    pack_rows(lse_ref, vst_ref, rows)

    @pl.loop(1, n_t)
    def _(k):
        pltpu.make_async_remote_copy(
            vst_ref.at[0], vst_ref.at[k], vs_send, vs_recv,
            device_id=(dp, lax.rem(t + k, n_t)), device_id_type=MESH).start()

    wait_bytes(sc_ref.at[pl.ds(0, rows - owned)], ag_recv)

    @pl.loop(0, chunks)
    def _(i):
        u_copy(i).wait()
        g_ref[:, columns(i)] = jnp.dot(
            sc_ref[...], u_ref[:, columns(i)], preferred_element_type=F32).astype(BF16)

    log_sum_rows(g_ref, rows, lse_ref)
    pack_rows(lse_ref, dst_ref, rows)

    @pl.loop(1, n_t)
    def _(k):
        pltpu.make_async_remote_copy(
            dst_ref.at[0], dst_ref.at[k], ds_send, ds_recv,
            device_id=(dp, lax.rem(t + k, n_t)), device_id_type=MESH).start()

    @pl.loop(0, depth // CHUNK)
    def _(i):
        tr_ref[columns(i), :] = jnp.transpose(sc_ref[:, columns(i)])

    def pt_copy(k):
        block = pl.ds(pl.multiple_of((2 * lax.rem(y + k, n_y) + 1 - core) * part, 16), part)
        return pltpu.make_async_remote_copy(
            tr_ref.at[block], pt_ref.at[pl.ds(k * part, part)], pt_send, pt_recv,
            device_id=partner, device_id_type=MESH)

    for k in range(n_y):
        pt_copy(k).start()
    for k in range(n_y):
        block = pl.ds(pl.multiple_of((2 * lax.rem(y + k, n_y) + core) * part, 16), part)
        ot_ref[k * part:(k + 1) * part, :] = tr_ref[block, :]

    wait_bytes(vst_ref.at[pl.ds(0, n_t - 1)], vs_recv)
    wait_bytes(dst_ref.at[pl.ds(0, n_t - 1)], ds_recv)
    log_weight = lw_ref[...]
    draft_off = combine(dst_ref) - log_weight
    verif_off = combine(vst_ref) - log_weight - jnp.log(F32(0.8))
    served = 0.2 * jnp.exp(log_weight)
    for b in range(rows // LANES):
        at = slice(b * LANES, (b + 1) * LANES)
        a_ref[at, :] = to_columns(draft_off[b:b + 1])
        b_ref[at, :] = to_columns(verif_off[b:b + 1])
        w_ref[at, :] = to_columns(served[b:b + 1])
        i_ref[at, :] = to_columns(ids_ref[b:b + 1, :] - t * width)

    lane = lax.broadcasted_iota(jnp.int32, (64, LANES), 1)

    def grads(i):
        for b in range(rows // 64):
            at = slice(b * 64, (b + 1) * 64)
            for j in range(CHUNK // LANES):
                col = pl.ds(pl.multiple_of(i * CHUNK + j * LANES, LANES), LANES)
                draft = jnp.exp(g_ref[at, col].astype(F32) - a_ref[at, :])
                verif = jnp.exp(v_ref[at, col].astype(F32) - b_ref[at, :])
                hit = i_ref[at, :] - (i * CHUNK + j * LANES) == lane
                g_ref[at, col] = (draft - verif - jnp.where(hit, w_ref[at, :], 0.0)).astype(BF16)

    def g_copy(i):
        return pltpu.make_async_remote_copy(
            g_ref.at[:, columns(i)], gp_ref.at[:, columns(i)], g_send, g_recv.at[i],
            device_id=partner, device_id_type=MESH)

    def left(i):
        return pl.ds(pl.multiple_of(i * CHUNK, LANES), LANES)

    def right(i):
        return pl.ds(pl.multiple_of(i * CHUNK + LANES, LANES), LANES)

    def slab(k):
        return pl.ds(k * part, part)

    def y_copy(k, col, dst_ref, sem, to):
        return pltpu.make_async_remote_copy(
            p_ref.at[slab(k), col], dst_ref.at[:, col], y_send, sem, device_id=to, device_id_type=MESH)

    def product(i):
        p_ref[:, columns(i)] = (
            jnp.dot(ot_ref[...], g_ref[:, columns(i)], preferred_element_type=F32)
            + jnp.dot(pt_ref[...], gp_ref[:, columns(i)], preferred_element_type=F32)).astype(BF16)

    def first_sends(i):
        y_copy(2, left(i), f_ref, f_recv.at[i, 0], down).start()
        y_copy(2, right(i), f_ref, f_recv.at[i, 1], up).start()
        y_copy(1, left(i), o_ref, o_recv, up).start()
        y_copy(3, right(i), o_ref, o_recv, down).start()

    grads(0)
    g_copy(0).start()
    wait_bytes(pt_ref, pt_recv)

    @pl.loop(1, chunks)
    def _(i):
        grads(i)
        g_copy(i).start()
        g_copy(i - 1).wait_recv()
        product(i - 1)
        first_sends(i - 1)

    g_copy(chunks - 1).wait_recv()
    product(chunks - 1)
    first_sends(chunks - 1)

    @pl.loop(0, depth // CHUNK)
    def _(n):
        block = pl.ds(pl.multiple_of(n * CHUNK, CHUNK), CHUNK)
        gn_ref[:, block] = lax.dot_general(
            g_ref[...], u_ref[block, :], (((1,), (1,)), ((), ())), preferred_element_type=F32).astype(BF16)

    @pl.loop(1, n_t)
    def _(k):
        peer = lax.rem(t + k, n_t)
        pltpu.make_async_remote_copy(
            gn_ref.at[pl.ds(pl.multiple_of(peer * owned, owned), owned)], gr_ref.at[k], n_send, n_recv,
            device_id=(dp, peer), device_id_type=MESH).start()

    def add_hop(i, side):
        k, col = (3, left(i)) if side == 0 else (1, right(i))
        p_ref[slab(k), col] = (p_ref[slab(k), col].astype(F32) + f_ref[:, col].astype(F32)).astype(BF16)
        y_copy(k, col, s_ref, s_recv.at[i, side], down if side == 0 else up).start()

    @pl.loop(0, chunks)
    def _(i):
        y_copy(2, left(i), f_ref, f_recv.at[i, 0], down).wait_recv()
        add_hop(i, 0)
        y_copy(2, right(i), f_ref, f_recv.at[i, 1], up).wait_recv()
        add_hop(i, 1)

    wait_bytes(gr_ref.at[pl.ds(0, n_t - 1)], n_recv)
    grad = gn_ref[own, :].astype(F32)
    for k in range(1, n_t):
        grad += gr_ref[k].astype(F32)
    hidden = hid_ref[...].astype(F32)
    inverse = lax.rsqrt(jnp.mean(hidden * hidden, axis=-1, keepdims=True) + 1e-06)
    normed = hidden * inverse
    grad = grad * gain_ref[...]
    inner = jnp.mean(grad * normed, axis=-1, keepdims=True)
    out_h[...] = (inverse * (grad - normed * inner)).astype(BF16)

    wait_bytes(o_ref, o_recv)

    @pl.loop(0, chunks)
    def _(i):
        y_copy(3, left(i), s_ref, s_recv.at[i, 0], down).wait_recv()
        y_copy(1, right(i), s_ref, s_recv.at[i, 1], up).wait_recv()
        cols = columns(i)
        out_u[:, cols] = (
            p_ref[slab(0), cols].astype(F32) + o_ref[:, cols].astype(F32) + s_ref[:, cols].astype(F32)).astype(BF16)

    wait_bytes(sc_ref.at[pl.ds(0, rows - owned)], ag_send)
    wait_bytes(vst_ref.at[pl.ds(0, n_t - 1)], vs_send)
    wait_bytes(dst_ref.at[pl.ds(0, n_t - 1)], ds_send)
    wait_bytes(pt_ref, pt_send)
    wait_bytes(g_ref, g_send)
    wait_bytes(p_ref.at[pl.ds(0, 3 * part)], y_send)
    wait_bytes(gr_ref.at[pl.ds(0, n_t - 1)], n_send)


def body(n_dp, n_t, hidden, norm_gain, unembed, verifier_logits, served_ids, accepted):
    owned, depth = hidden.shape
    rows, width = verifier_logits.shape
    part = depth // n_dp
    chunks = width // CHUNK
    slot = jnp.arange(rows, dtype=jnp.int32) % DRAFT
    log_weight = jnp.where(slot <= jnp.repeat(accepted, DRAFT), 0.0, jnp.log(F32(0.2))).astype(F32)
    pad = ((0, 8 - rows // LANES), (0, 0))
    log_weight = jnp.pad(log_weight.reshape(rows // LANES, LANES), pad)
    ids = jnp.pad(served_ids.reshape(rows // LANES, LANES), pad)
    vmem = pl.BlockSpec(memory_space=pltpu.VMEM)
    hbm = pl.BlockSpec(memory_space=pl.ANY)
    dma = pltpu.SemaphoreType.DMA
    return pl.pallas_call(
        functools.partial(kernel, n_dp, n_t),
        out_shape=(
            jax.ShapeDtypeStruct((part, width), BF16),
            jax.ShapeDtypeStruct((owned, depth), BF16),
        ),
        in_specs=[vmem, vmem, hbm, hbm, vmem, vmem],
        out_specs=(vmem, vmem),
        scratch_shapes=[
            pltpu.VMEM((depth, width), BF16),
            pltpu.VMEM((rows, width), BF16),
            pltpu.VMEM((rows, width), BF16),
            pltpu.VMEM((rows, width), BF16),
            pltpu.VMEM((rows, depth), BF16),
            pltpu.VMEM((depth, rows), BF16),
            pltpu.VMEM((depth // 2, rows), BF16),
            pltpu.VMEM((depth // 2, rows), BF16),
            pltpu.VMEM((depth // 2, width), BF16),
            pltpu.VMEM((part, width), BF16),
            pltpu.VMEM((part, width), BF16),
            pltpu.VMEM((part, width), BF16),
            pltpu.VMEM((rows, depth), BF16),
            pltpu.VMEM((n_t, owned, depth), BF16),
            pltpu.VMEM((rows, LANES), F32),
            pltpu.VMEM((rows, LANES), F32),
            pltpu.VMEM((rows, LANES), F32),
            pltpu.VMEM((rows, LANES), jnp.int32),
            pltpu.VMEM((rows, LANES), F32),
            pltpu.VMEM((n_t, 8, LANES), F32),
            pltpu.VMEM((n_t, 8, LANES), F32),
            dma, dma((chunks,)), dma, dma, dma, dma, dma, dma, dma, dma,
            dma, dma((chunks,)), dma, dma((chunks, 2)), dma, dma((chunks, 2)), dma, dma,
        ],
        compiler_params=pltpu.CompilerParams(
            collective_id=0, has_side_effects=True, vmem_limit_bytes=62 * 1024 * 1024),
        cost_estimate=pl.CostEstimate(
            flops=6 * rows * depth * width, bytes_accessed=2 * (depth + rows + part) * width,
            transcendentals=4 * rows * width),
    )(hidden, norm_gain.reshape(1, depth), unembed, verifier_logits, ids, log_weight)


def solution(mesh):
    n_dp, n_t = mesh.shape["dp"], mesh.shape["tensor"]

    def run(*args):
        return body(n_dp, n_t, *args)

    return jax.shard_map(
        run,
        mesh=mesh,
        in_specs=(
            P(("dp", "tensor"), None),
            P(),
            P(None, "tensor"),
            P("dp", "tensor"),
            P("dp"),
            P("dp"),
        ),
        out_specs=(P("dp", "tensor"), P(("dp", "tensor"), None)),
        check_vma=False,
    )
```

time: 452 us -> 127 us (0.28)
  waiting for transfers between devices: 290 us -> 0 us
  Pallas kernels: 0 us -> 118 us
  blocking collectives: 61.5 us -> 0 us
  matrix products: 41 us -> 0 us
  other arithmetic: 27.2 us -> 0.01 us
  starting transfers between devices: 13.3 us -> 0 us
  between operations: 13.8 us -> 0.65 us
    reduce_scatter x2 -> x0, waiting for transfers between devices: 143 us -> none  [the longest x1 84.2 us: body(): lax.psum_scatter(lax.dot_general(scaled, grad_logits, (((0,), (0,)), ((),...]
    pallas_call x0 -> x1, Pallas kernels: none -> 118 us  [body(): pl.pallas_call(functools.partial(kernel, n_dp, n_t), out_shape=(jax.Shape...]
    all_gather x1 -> x0, waiting for transfers between devices: 84.3 us -> none  [body(): group_hidden = lax.all_gather(hidden, 'tensor', axis=0, tiled=True)]
    all_to_all x2 -> x0, waiting for transfers between devices: 62.6 us -> none  [the longest x1 62.6 us: body(): lax.all_to_all(drafter, 'tensor', split_axis=0, concat_axis=1, tiled=True)]
    all_to_all x1 -> x0, blocking collectives: 61.5 us -> none  [body(): lax.all_to_all(owner_grads, 'tensor', split_axis=1, concat_axis=0, tiled=...]
    dot_general x3 -> x0, matrix products: 41 us -> none  [the longest x1 15.3 us: body(): jnp.dot(scaled, unembed, preferred_element_type=jnp.float32)]
    all_to_all x2 -> x0, starting transfers between devices: 13.2 us -> none  [the longest x1 8.48 us: body(): lax.all_to_all(verifier_logits, 'tensor', split_axis=0, concat_axis=1, ti...]
    reduce_sum x5 -> x0, other arithmetic: 11.4 us -> none  [the longest x2 8.39 us: totals(): return (top, jnp.sum(jnp.exp(logits - top[:, None]), axis=-1))]
  transfers between devices with their start and end apart: 5 -> 0, of which waited for: 4 -> 0; matrix products, arithmetic and copies ran while one was open for 9% -> 0% of each run, Pallas kernels for 0% -> 0%
where the time goes in v1:
time: 127 us
  Pallas kernels  118 us (93%)
  local copies, waits for them, and re-layouts  8.47 us (7%)
    pallas_call x1, Pallas kernels, body(): pl.pallas_call(functools.partial(kernel, n_dp, n_t), out_shape=(jax.Shape...  118 us
    unnamed x2, local copies, waits for them, and re-layouts  4.41 us

profile of v1, /device:TPU:1, one launch (start us, length us, event | category | flops | bytes accessed | tf_op | source)
XLA Modules:
  0.0 126.8 jit_solution(902947527790930990)
XLA Ops:
  0.6 0.7 broadcast_in_dim.15
  1.4 1.3 %pad.8.ids_ref = s32[8,128]{1,0:T(8,128)} pad(s32[4,128]{1,0:T(4,128)} %bitcast.1, s32[]{:T(128)} %constant.17.clone.1), padding=0_4x0_0 | pad | bytes 6148 | tf_op jit(solution)/shard_map/jit(_pad)/pad | solution.py:287
  2.6 1.3 %reshape.16.gain_ref = f32[1,1536]{1,0:T(1,128)} reshape(f32[1536]{0:T(1024)} %param.7) | data formatting | bytes 12288 | tf_op jit(solution)/shard_map/reshape | solution.py:329
  3.9 0.1 broadcast_in_dim.16
  4.0 0.1 broadcast_in_dim.17
  4.1 0.6 pad.9.lw_ref
  4.7 117.7 %shard_map.77 = (bf16[192,4864]{1,0:T(8,128)(2,1)}, bf16[32,1536]{1,0:T(8,128)(2,1)}) custom-call(bf16[32,1536]{1,0:T(8,128)(2,1)} %hid_ref.1, f32[1,1536]{1,0:T(1,128)} %reshape.16.gain_ref, bf16[1536,4864]{1,0:T(8,128)(2,1)} %u_hbm.1, bf16[512,4864]{1,0:T(8,128)(2,1)} %v_hbm.1, s32[8,128]{1,0:T(8,128)} %pad.8.ids_ref, f32[8,128]{1,0:T(8,128)} %pad.9.lw_ref), custom_call_target="tpu_custom_call" | custom-call | flops 22951231488 | bytes 21790720 | tf_op jit(solution)/shard_map/pallas_call | solution.py:291
  122.4 2.9 %copy.10 = bf16[192,4864]{1,0:T(8,128)(2,1)} copy(bf16[192,4864]{1,0:T(8,128)(2,1)} %get-tuple-element.4) | data formatting | bytes 3735552
  125.3 1.5 %copy.11 = bf16[32,1536]{1,0:T(8,128)(2,1)} copy(bf16[32,1536]{1,0:T(8,128)(2,1)} %get-tuple-element.5) | data formatting | bytes 196608
  (1 shorter events, 0.0 us)

commit v2 on v1

--- a/solution.py
+++ b/solution.py
@@ -8,6 +8,8 @@
 from jax.sharding import PartitionSpec as P
 
 DRAFT = 8
+SIDE = 4
+LOG_LOW = -1.6094379124341003
 MESH = pl.DeviceIdType.MESH
 F32 = jnp.float32
 BF16 = jnp.bfloat16
@@ -23,23 +25,19 @@
     return jnp.transpose(jnp.broadcast_to(row, (LANES, LANES)))
 
 
-def log_sum_rows(ref, rows, lse_ref):
-    block, width = 64, ref.shape[1]
-
-    @pl.loop(0, rows // block)
-    def _(index):
-        at = pl.ds(pl.multiple_of(index * block, block), block)
-        tops = [ref[at, j * LANES:(j + 1) * LANES].astype(F32) for j in range(4)]
-        for j in range(4, width // LANES):
-            tops[j % 4] = jnp.maximum(tops[j % 4], ref[at, j * LANES:(j + 1) * LANES].astype(F32))
-        top = jnp.maximum(jnp.maximum(tops[0], tops[1]), jnp.maximum(tops[2], tops[3]))
-        top = jnp.max(top, axis=-1, keepdims=True)
-        wide = jnp.broadcast_to(top, (block, LANES))
-        sums = [jnp.zeros((block, LANES), F32) for _ in range(2)]
-        for j in range(width // LANES):
-            sums[j % 2] += jnp.exp(ref[at, j * LANES:(j + 1) * LANES].astype(F32) - wide)
-        total = jnp.sum(sums[0] + sums[1], axis=-1, keepdims=True)
-        lse_ref[at, :] = jnp.broadcast_to(top + jnp.log(total), (block, LANES))
+def log_sum_rows(ref, index, lse_ref):
+    block, width = 32, ref.shape[1]
+    at = pl.ds(pl.multiple_of(index * block, block), block)
+    tops = [ref[at, j * LANES:(j + 1) * LANES].astype(F32) for j in range(2)]
+    for j in range(2, width // LANES):
+        tops[j % 2] = jnp.maximum(tops[j % 2], ref[at, j * LANES:(j + 1) * LANES].astype(F32))
+    top = jnp.max(jnp.maximum(tops[0], tops[1]), axis=-1, keepdims=True)
+    wide = jnp.broadcast_to(top, (block, LANES))
+    sums = [jnp.zeros((block, LANES), F32) for _ in range(2)]
+    for j in range(width // LANES):
+        sums[j % 2] += jnp.exp(ref[at, j * LANES:(j + 1) * LANES].astype(F32) - wide)
+    total = jnp.sum(sums[0] + sums[1], axis=-1, keepdims=True)
+    lse_ref[at, :] = jnp.broadcast_to(top + jnp.log(total), (block, LANES))
 
 
 def pack_rows(lse_ref, stat_ref, rows):
@@ -55,10 +53,10 @@
     return top + jnp.log(jnp.sum(jnp.exp(stats - top[None]), axis=0))
 
 
-def kernel(n_dp, n_t, hid_ref, gain_ref, u_hbm, v_hbm, ids_ref, lw_ref, out_u, out_h,
+def kernel(n_dp, n_t, hid_ref, gain_ref, u_hbm, v_hbm, ids_ref, acc_ref, out_u, out_h,
            u_ref, v_ref, g_ref, gp_ref, sc_ref, tr_ref, ot_ref, pt_ref, p_ref, f_ref, o_ref, s_ref,
-           gn_ref, gr_ref, lse_ref, a_ref, b_ref, i_ref, w_ref, vst_ref, dst_ref,
-           v_sem, u_sem, ag_send, ag_recv, vs_send, vs_recv, ds_send, ds_recv, pt_send, pt_recv,
+           gn_ref, gr_ref, lse_ref, a_ref, b_ref, i_ref, w_ref, lw_ref, m_ref, z_ref, vst_ref, dst_ref,
+           v_sem, u_sem, ag_send, r1_sem, r2_sem, r3_sem, vs_send, vs_recv, ds_send, ds_recv, pt_send, pt_recv,
            g_send, g_recv, y_send, f_recv, o_recv, s_recv, n_send, n_recv):
     rows, width = v_ref.shape
     owned, depth = hid_ref.shape
@@ -93,22 +91,121 @@
     for other in (partner, up, down):
         pl.semaphore_signal(barrier, inc=1, device_id=other, device_id_type=MESH)
 
+    z, x = t // SIDE, lax.rem(t, SIDE)
+    place = (x, z)
+
+    def first_axis(half, off):
+        if half == 0:
+            return (dp, z * SIDE + lax.rem(x + off, SIDE))
+        return (dp, lax.rem(z + off, SIDE) * SIDE + x)
+
+    def second_axis(half, off):
+        return first_axis(1 - half, off)
+
+    def line_copy(half, off):
+        block = sc_ref.at[0, half, place[half]]
+        return pltpu.make_async_remote_copy(
+            block, block, ag_send, r1_sem.at[half, off],
+            device_id=first_axis(half, off), device_id_type=MESH)
+
+    def cross_copy(half, off, back):
+        o = lax.rem(place[half] + SIDE - off, SIDE)
+        return pltpu.make_async_remote_copy(
+            sc_ref.at[0, half, o], sc_ref.at[1 if back else 2, half, o], ag_send, r2_sem.at[half, off, back],
+            device_id=second_axis(half, SIDE - 1 if back else 1), device_id_type=MESH)
+
+    def relay_copy(half, off, back):
+        o = lax.rem(place[half] + SIDE - off, SIDE)
+        cols = pl.ds(depth // 2, depth // 2) if back else pl.ds(0, depth // 2)
+        return pltpu.make_async_remote_copy(
+            sc_ref.at[1 if back else 2, half, o, :, cols], sc_ref.at[3, half, o, :, cols], ag_send, r3_sem,
+            device_id=second_axis(half, SIDE - 1 if back else 1), device_id_type=MESH)
+
     hidden = hid_ref[...].astype(F32)
     inverse = lax.rsqrt(jnp.mean(hidden * hidden, axis=-1, keepdims=True) + 1e-06)
-    own = pl.ds(pl.multiple_of(t * owned, owned), owned)
-    sc_ref[own, :] = (hidden * inverse * gain_ref[...]).astype(BF16)
+    scaled = (hidden * inverse * gain_ref[...][None, :]).astype(BF16)
+    for half in range(2):
+        sc_ref[0, half, place[half]] = scaled[half * owned // 2:(half + 1) * owned // 2]
     pl.semaphore_wait(barrier, n_t + 2)
 
-    @pl.loop(1, n_t)
-    def _(k):
-        pltpu.make_async_remote_copy(
-            sc_ref.at[own], sc_ref.at[own], ag_send, ag_recv,
-            device_id=(dp, lax.rem(t + k, n_t)), device_id_type=MESH).start()
-
-    v_copy.wait()
-    log_sum_rows(v_ref, rows, lse_ref)
+    for off in (1, 3, 2):
+        for half in range(2):
+            line_copy(half, off).start()
+    for half in range(2):
+        for back in range(2):
+            cross_copy(half, 0, back).start()
+
+    m_ref[...] = jnp.full(m_ref.shape, -jnp.inf, F32)
+    z_ref[...] = jnp.zeros(z_ref.shape, F32)
     vst_ref[0] = jnp.zeros(vst_ref.shape[1:], F32)
     dst_ref[0] = jnp.zeros(dst_ref.shape[1:], F32)
+    blocks = rows // DRAFT
+    for b in range(rows // LANES):
+        at = slice(b * LANES, (b + 1) * LANES)
+        row = b * LANES + lax.broadcasted_iota(jnp.int32, (LANES, blocks), 0)
+        same = lax.shift_right_logical(row, 3) == lax.broadcasted_iota(jnp.int32, (LANES, blocks), 1)
+        count = jnp.sum(jnp.where(same, acc_ref[...].astype(F32), 0.0), axis=-1, keepdims=True)
+        slot = (lax.broadcasted_iota(jnp.int32, (LANES, LANES), 0) & (DRAFT - 1)).astype(F32)
+        kept = slot <= jnp.broadcast_to(count, (LANES, LANES))
+        lw_ref[at, :] = jnp.where(kept, 0.0, LOG_LOW)
+        w_ref[at, :] = jnp.where(kept, 0.2, 0.2 * 0.2)
+        i_ref[at, :] = to_columns(ids_ref[b:b + 1, :] - t * width)
+
+    def forward_cross(off):
+        for half in range(2):
+            line_copy(half, off).wait_recv()
+            for back in range(2):
+                cross_copy(half, off, back).start()
+
+    def forward_relay(off):
+        for half in range(2):
+            for back in range(2):
+                cross_copy(half, off, back).wait_recv()
+                relay_copy(half, off, back).start()
+
+    forward_cross(1)
+    forward_cross(3)
+    forward_relay(0)
+    forward_cross(2)
+    for off in (1, 3, 2):
+        forward_relay(off)
+    v_copy.wait()
+
+    quarter = rows // SIDE
+
+    def home(block):
+        slot, half, o = block // 8, block // 4 % 2, block % 4
+        far = lax.rem(place[1 - half] + (0, 1, SIDE - 1, 2)[slot], SIDE)
+        if half == 0:
+            return pl.multiple_of(far * quarter + o * owned, 16)
+        return pl.multiple_of(o * quarter + far * owned + 16, 16)
+
+    def drafter(i, lo, hi):
+        count = (hi - lo) * quarter
+        logits = jnp.dot(
+            sc_ref[lo:hi].reshape(count, depth), u_ref[:, columns(i)], preferred_element_type=F32).astype(BF16)
+        for b in range(count // 16):
+            g_ref[pl.ds(home(lo * 8 + b), 16), columns(i)] = logits[b * 16:(b + 1) * 16]
+        for b in range(count // 32):
+            at = slice(lo * quarter + b * 32, lo * quarter + (b + 1) * 32)
+            piece = logits[b * 32:(b + 1) * 32].astype(F32)
+            tiles = [piece[:, j * LANES:(j + 1) * LANES] for j in range(CHUNK // LANES)]
+            old = m_ref[at, :]
+            top = old
+            for tile in tiles:
+                top = jnp.maximum(top, tile)
+            total = z_ref[at, :] * jnp.exp(old - top)
+            for tile in tiles:
+                total += jnp.exp(tile - top)
+            m_ref[at, :] = top
+            z_ref[at, :] = total
+
+    @pl.loop(0, chunks)
+    def _(i):
+        u_copy(i).wait()
+        drafter(i, 0, 3)
+        log_sum_rows(v_ref, jnp.minimum(i, rows // 32 - 1), lse_ref)
+
     pack_rows(lse_ref, vst_ref, rows)
 
     @pl.loop(1, n_t)
@@ -117,15 +214,17 @@
             vst_ref.at[0], vst_ref.at[k], vs_send, vs_recv,
             device_id=(dp, lax.rem(t + k, n_t)), device_id_type=MESH).start()
 
-    wait_bytes(sc_ref.at[pl.ds(0, rows - owned)], ag_recv)
+    wait_bytes(sc_ref.at[3], r3_sem)
 
     @pl.loop(0, chunks)
     def _(i):
-        u_copy(i).wait()
-        g_ref[:, columns(i)] = jnp.dot(
-            sc_ref[...], u_ref[:, columns(i)], preferred_element_type=F32).astype(BF16)
-
-    log_sum_rows(g_ref, rows, lse_ref)
+        drafter(i, 3, 4)
+
+    for b in range(rows // 16):
+        at = slice(b * 16, (b + 1) * 16)
+        top = jnp.max(m_ref[at, :], axis=-1, keepdims=True)
+        total = jnp.sum(z_ref[at, :] * jnp.exp(m_ref[at, :] - top), axis=-1, keepdims=True)
+        lse_ref[pl.ds(home(b), 16), :] = jnp.broadcast_to(top + jnp.log(total), (16, LANES))
     pack_rows(lse_ref, dst_ref, rows)
 
     @pl.loop(1, n_t)
@@ -134,9 +233,12 @@
             dst_ref.at[0], dst_ref.at[k], ds_send, ds_recv,
             device_id=(dp, lax.rem(t + k, n_t)), device_id_type=MESH).start()
 
+    for b in range(rows // 16):
+        gn_ref[pl.ds(home(b), 16), :] = sc_ref[b // 8, b // 4 % 2, b % 4]
+
     @pl.loop(0, depth // CHUNK)
     def _(i):
-        tr_ref[columns(i), :] = jnp.transpose(sc_ref[:, columns(i)])
+        tr_ref[columns(i), :] = jnp.transpose(gn_ref[:, columns(i)])
 
     def pt_copy(k):
         block = pl.ds(pl.multiple_of((2 * lax.rem(y + k, n_y) + 1 - core) * part, 16), part)
@@ -151,17 +253,15 @@
         ot_ref[k * part:(k + 1) * part, :] = tr_ref[block, :]
 
     wait_bytes(vst_ref.at[pl.ds(0, n_t - 1)], vs_recv)
-    wait_bytes(dst_ref.at[pl.ds(0, n_t - 1)], ds_recv)
-    log_weight = lw_ref[...]
-    draft_off = combine(dst_ref) - log_weight
-    verif_off = combine(vst_ref) - log_weight - jnp.log(F32(0.8))
-    served = 0.2 * jnp.exp(log_weight)
+    verif_off = combine(vst_ref) - jnp.log(F32(0.8))
     for b in range(rows // LANES):
         at = slice(b * LANES, (b + 1) * LANES)
-        a_ref[at, :] = to_columns(draft_off[b:b + 1])
-        b_ref[at, :] = to_columns(verif_off[b:b + 1])
-        w_ref[at, :] = to_columns(served[b:b + 1])
-        i_ref[at, :] = to_columns(ids_ref[b:b + 1, :] - t * width)
+        b_ref[at, :] = to_columns(verif_off[b:b + 1]) - lw_ref[at, :]
+    wait_bytes(dst_ref.at[pl.ds(0, n_t - 1)], ds_recv)
+    draft_off = combine(dst_ref)
+    for b in range(rows // LANES):
+        at = slice(b * LANES, (b + 1) * LANES)
+        a_ref[at, :] = to_columns(draft_off[b:b + 1]) - lw_ref[at, :]
 
     lane = lax.broadcasted_iota(jnp.int32, (64, LANES), 1)
 
@@ -246,13 +346,14 @@
         add_hop(i, 1)
 
     wait_bytes(gr_ref.at[pl.ds(0, n_t - 1)], n_recv)
+    own = pl.ds(pl.multiple_of(t * owned, owned), owned)
     grad = gn_ref[own, :].astype(F32)
     for k in range(1, n_t):
         grad += gr_ref[k].astype(F32)
     hidden = hid_ref[...].astype(F32)
     inverse = lax.rsqrt(jnp.mean(hidden * hidden, axis=-1, keepdims=True) + 1e-06)
     normed = hidden * inverse
-    grad = grad * gain_ref[...]
+    grad = grad * gain_ref[...][None, :]
     inner = jnp.mean(grad * normed, axis=-1, keepdims=True)
     out_h[...] = (inverse * (grad - normed * inner)).astype(BF16)
 
@@ -266,7 +367,8 @@
         out_u[:, cols] = (
             p_ref[slab(0), cols].astype(F32) + o_ref[:, cols].astype(F32) + s_ref[:, cols].astype(F32)).astype(BF16)
 
-    wait_bytes(sc_ref.at[pl.ds(0, rows - owned)], ag_send)
+    for part_sent in (sc_ref.at[0], sc_ref.at[0], sc_ref.at[3], sc_ref.at[0, 0, pl.ds(0, 3)], sc_ref.at[0, 0, pl.ds(0, 3)]):
+        wait_bytes(part_sent, ag_send)
     wait_bytes(vst_ref.at[pl.ds(0, n_t - 1)], vs_send)
     wait_bytes(dst_ref.at[pl.ds(0, n_t - 1)], ds_send)
     wait_bytes(pt_ref, pt_send)
@@ -280,11 +382,6 @@
     rows, width = verifier_logits.shape
     part = depth // n_dp
     chunks = width // CHUNK
-    slot = jnp.arange(rows, dtype=jnp.int32) % DRAFT
-    log_weight = jnp.where(slot <= jnp.repeat(accepted, DRAFT), 0.0, jnp.log(F32(0.2))).astype(F32)
-    pad = ((0, 8 - rows // LANES), (0, 0))
-    log_weight = jnp.pad(log_weight.reshape(rows // LANES, LANES), pad)
-    ids = jnp.pad(served_ids.reshape(rows // LANES, LANES), pad)
     vmem = pl.BlockSpec(memory_space=pltpu.VMEM)
     hbm = pl.BlockSpec(memory_space=pl.ANY)
     dma = pltpu.SemaphoreType.DMA
@@ -301,7 +398,7 @@
             pltpu.VMEM((rows, width), BF16),
             pltpu.VMEM((rows, width), BF16),
             pltpu.VMEM((rows, width), BF16),
-            pltpu.VMEM((rows, depth), BF16),
+            pltpu.VMEM((SIDE, 2, SIDE, owned // 2, depth), BF16),
             pltpu.VMEM((depth, rows), BF16),
             pltpu.VMEM((depth // 2, rows), BF16),
             pltpu.VMEM((depth // 2, rows), BF16),
@@ -316,9 +413,12 @@
             pltpu.VMEM((rows, LANES), F32),
             pltpu.VMEM((rows, LANES), jnp.int32),
             pltpu.VMEM((rows, LANES), F32),
+            pltpu.VMEM((rows, LANES), F32),
+            pltpu.VMEM((rows, LANES), F32),
+            pltpu.VMEM((rows, LANES), F32),
             pltpu.VMEM((n_t, 8, LANES), F32),
             pltpu.VMEM((n_t, 8, LANES), F32),
-            dma, dma((chunks,)), dma, dma, dma, dma, dma, dma, dma, dma,
+            dma, dma((chunks,)), dma, dma((2, SIDE)), dma((2, SIDE, 2)), dma, dma, dma, dma, dma, dma, dma,
             dma, dma((chunks,)), dma, dma((chunks, 2)), dma, dma((chunks, 2)), dma, dma,
         ],
         compiler_params=pltpu.CompilerParams(
@@ -326,7 +426,7 @@
         cost_estimate=pl.CostEstimate(
             flops=6 * rows * depth * width, bytes_accessed=2 * (depth + rows + part) * width,
             transcendentals=4 * rows * width),
-    )(hidden, norm_gain.reshape(1, depth), unembed, verifier_logits, ids, log_weight)
+    )(hidden, norm_gain, unembed, verifier_logits, served_ids.reshape(rows // LANES, LANES), accepted.reshape(1, rows // DRAFT))
 
 
 def solution(mesh):

time: 127 us -> 112 us (0.88)
  Pallas kernels: 118 us -> 107 us
  local copies, waits for them, and re-layouts: 8.47 us -> 4.41 us
    pallas_call x1, Pallas kernels: 118 us -> 107 us  [body(): pl.pallas_call(functools.partial(kernel, n_dp, n_t), out_shape=(jax.Shape...]
    pad x2 -> x0, local copies, waits for them, and re-layouts: 1.87 us -> none  [the longest x1 1.28 us: body(): ids = jnp.pad(served_ids.reshape(rows // LANES, LANES), pad)]
    reshape x1 -> x0, local copies, waits for them, and re-layouts: 1.29 us -> none  [body(): norm_gain.reshape(1, depth)]
where the time goes in v2:
time: 112 us
  Pallas kernels  107 us (96%)
  local copies, waits for them, and re-layouts  4.41 us (4%)
    pallas_call x1, Pallas kernels, body(): pl.pallas_call(functools.partial(kernel, n_dp, n_t), out_shape=(jax.Shape...  107 us
    unnamed x2, local copies, waits for them, and re-layouts  4.41 us

profile of v2, /device:TPU:1, one launch (start us, length us, event | category | flops | bytes accessed | tf_op | source)
XLA Modules:
  0.0 111.9 jit_solution(13234942992546541954)
XLA Ops:
  0.6 106.9 %shard_map.77 = (bf16[192,4864]{1,0:T(8,128)(2,1)}, bf16[32,1536]{1,0:T(8,128)(2,1)}) custom-call(bf16[32,1536]{1,0:T(8,128)(2,1)} %hid_ref.1, f32[1536]{0:T(1024)} %gain_ref.1, bf16[1536,4864]{1,0:T(8,128)(2,1)} %u_hbm.1, bf16[512,4864]{1,0:T(8,128)(2,1)} %v_hbm.1, s32[4,128]{1,0:T(4,128)} %bitcast.2, s32[1,64]{1,0:T(1,128)} %bitcast.3), custom_call_target="tpu_custom_call" | custom-call | flops 22951231488 | bytes 21790720 | tf_op jit(solution)/shard_map/pallas_call | solution.py:388
  107.5 2.9 %copy.10 = bf16[192,4864]{1,0:T(8,128)(2,1)} copy(bf16[192,4864]{1,0:T(8,128)(2,1)} %get-tuple-element.4) | data formatting | bytes 3735552
  110.4 1.5 %copy.11 = bf16[32,1536]{1,0:T(8,128)(2,1)} copy(bf16[32,1536]{1,0:T(8,128)(2,1)} %get-tuple-element.5) | data formatting | bytes 196608

commit v3 on v2

--- a/solution.py
+++ b/solution.py
@@ -9,6 +9,7 @@
 
 DRAFT = 8
 SIDE = 4
+WAVES = 1
 LOG_LOW = -1.6094379124341003
 MESH = pl.DeviceIdType.MESH
 F32 = jnp.float32
@@ -53,15 +54,15 @@
     return top + jnp.log(jnp.sum(jnp.exp(stats - top[None]), axis=0))
 
 
-def kernel(n_dp, n_t, hid_ref, gain_ref, u_hbm, v_hbm, ids_ref, acc_ref, out_u, out_h,
-           u_ref, v_ref, g_ref, gp_ref, sc_ref, tr_ref, ot_ref, pt_ref, p_ref, f_ref, o_ref, s_ref,
+def kernel(n_dp, n_t, hid_ref, gain_ref, u_hbm, v_hbm, ids_ref, acc_ref, out_a, out_s, out_h,
+           even_ref, odd_ref, u_ref, v_ref, g_ref, gp_ref, sc_ref, tr_ref, ot_ref, pt_ref, p_ref, f_ref, o_ref,
            gn_ref, gr_ref, lse_ref, a_ref, b_ref, i_ref, w_ref, lw_ref, m_ref, z_ref, vst_ref, dst_ref,
            v_sem, u_sem, ag_send, r1_sem, r2_sem, r3_sem, vs_send, vs_recv, ds_send, ds_recv, pt_send, pt_recv,
-           g_send, g_recv, y_send, f_recv, o_recv, s_recv, n_send, n_recv):
+           g_send, g_recv, y_send, f_recv, o_recv, s_recv, a_sem, n_send, n_recv):
     rows, width = v_ref.shape
     owned, depth = hid_ref.shape
     chunks = width // CHUNK
-    part = out_u.shape[0]
+    part = out_a.shape[0]
     n_y = n_dp // 2
     dp, t = lax.axis_index("dp"), lax.axis_index("tensor")
     y, core = dp // 2, lax.rem(dp, 2)
@@ -102,24 +103,56 @@
     def second_axis(half, off):
         return first_axis(1 - half, off)
 
-    def line_copy(half, off):
-        block = sc_ref.at[0, half, place[half]]
+    span = depth // WAVES
+
+    def line_copy(w, half, off):
+        block = sc_ref.at[0, half, place[half], :, pl.ds(w * span, span)]
         return pltpu.make_async_remote_copy(
-            block, block, ag_send, r1_sem.at[half, off],
+            block, block, ag_send, r1_sem.at[w, half, off],
             device_id=first_axis(half, off), device_id_type=MESH)
 
-    def cross_copy(half, off, back):
+    def cross_copy(w, half, off, back):
         o = lax.rem(place[half] + SIDE - off, SIDE)
+        cols = pl.ds(w * span, span)
         return pltpu.make_async_remote_copy(
-            sc_ref.at[0, half, o], sc_ref.at[1 if back else 2, half, o], ag_send, r2_sem.at[half, off, back],
+            sc_ref.at[0, half, o, :, cols], sc_ref.at[1 if back else 2, half, o, :, cols],
+            ag_send, r2_sem.at[w, half, off, back],
             device_id=second_axis(half, SIDE - 1 if back else 1), device_id_type=MESH)
 
-    def relay_copy(half, off, back):
+    def relay_copy(w, half, off, back):
         o = lax.rem(place[half] + SIDE - off, SIDE)
-        cols = pl.ds(depth // 2, depth // 2) if back else pl.ds(0, depth // 2)
+        cols = pl.ds(w * span + back * span // 2, span // 2)
         return pltpu.make_async_remote_copy(
-            sc_ref.at[1 if back else 2, half, o, :, cols], sc_ref.at[3, half, o, :, cols], ag_send, r3_sem,
+            sc_ref.at[1 if back else 2, half, o, :, cols], sc_ref.at[3, half, o, :, cols], ag_send, r3_sem.at[w],
             device_id=second_axis(half, SIDE - 1 if back else 1), device_id_type=MESH)
+
+    def begin(w):
+        for off in (1, 3, 2):
+            for half in range(2):
+                line_copy(w, half, off).start()
+        for half in range(2):
+            for back in range(2):
+                cross_copy(w, half, 0, back).start()
+
+    def forward_cross(w, off):
+        for half in range(2):
+            line_copy(w, half, off).wait_recv()
+            for back in range(2):
+                cross_copy(w, half, off, back).start()
+
+    def forward_relay(w, off):
+        for half in range(2):
+            for back in range(2):
+                cross_copy(w, half, off, back).wait_recv()
+                relay_copy(w, half, off, back).start()
+
+    def gathered(w):
+        wait_bytes(sc_ref.at[3, :, :, :, pl.ds(w * span, span)], r3_sem.at[w])
+
+    def verifier(first, last):
+        @pl.loop(first, last)
+        def _(i):
+            log_sum_rows(v_ref, i, lse_ref)
 
     hidden = hid_ref[...].astype(F32)
     inverse = lax.rsqrt(jnp.mean(hidden * hidden, axis=-1, keepdims=True) + 1e-06)
@@ -128,13 +161,7 @@
         sc_ref[0, half, place[half]] = scaled[half * owned // 2:(half + 1) * owned // 2]
     pl.semaphore_wait(barrier, n_t + 2)
 
-    for off in (1, 3, 2):
-        for half in range(2):
-            line_copy(half, off).start()
-    for half in range(2):
-        for back in range(2):
-            cross_copy(half, 0, back).start()
-
+    begin(0)
     m_ref[...] = jnp.full(m_ref.shape, -jnp.inf, F32)
     z_ref[...] = jnp.zeros(z_ref.shape, F32)
     vst_ref[0] = jnp.zeros(vst_ref.shape[1:], F32)
@@ -151,25 +178,33 @@
         w_ref[at, :] = jnp.where(kept, 0.2, 0.2 * 0.2)
         i_ref[at, :] = to_columns(ids_ref[b:b + 1, :] - t * width)
 
-    def forward_cross(off):
-        for half in range(2):
-            line_copy(half, off).wait_recv()
-            for back in range(2):
-                cross_copy(half, off, back).start()
-
-    def forward_relay(off):
-        for half in range(2):
-            for back in range(2):
-                cross_copy(half, off, back).wait_recv()
-                relay_copy(half, off, back).start()
-
-    forward_cross(1)
-    forward_cross(3)
-    forward_relay(0)
-    forward_cross(2)
-    for off in (1, 3, 2):
-        forward_relay(off)
     v_copy.wait()
+    forward_cross(0, 1)
+    forward_cross(0, 3)
+    verifier(0, 3)
+    forward_relay(0, 0)
+    verifier(3, 6)
+    forward_cross(0, 2)
+    verifier(6, 9)
+    forward_relay(0, 1)
+    verifier(9, 11)
+    forward_relay(0, 3)
+    verifier(11, 13)
+    forward_relay(0, 2)
+    verifier(13, rows // 32)
+    pack_rows(lse_ref, vst_ref, rows)
+
+    @pl.loop(1, n_t)
+    def _(k):
+        pltpu.make_async_remote_copy(
+            vst_ref.at[0], vst_ref.at[k], vs_send, vs_recv,
+            device_id=(dp, lax.rem(t + k, n_t)), device_id_type=MESH).start()
+
+    gathered(0)
+
+    @pl.loop(0, chunks)
+    def _(i):
+        u_copy(i).wait()
 
     quarter = rows // SIDE
 
@@ -180,15 +215,16 @@
             return pl.multiple_of(far * quarter + o * owned, 16)
         return pl.multiple_of(o * quarter + far * owned + 16, 16)
 
-    def drafter(i, lo, hi):
-        count = (hi - lo) * quarter
-        logits = jnp.dot(
-            sc_ref[lo:hi].reshape(count, depth), u_ref[:, columns(i)], preferred_element_type=F32).astype(BF16)
-        for b in range(count // 16):
-            g_ref[pl.ds(home(lo * 8 + b), 16), columns(i)] = logits[b * 16:(b + 1) * 16]
-        for b in range(count // 32):
-            at = slice(lo * quarter + b * 32, lo * quarter + (b + 1) * 32)
-            piece = logits[b * 32:(b + 1) * 32].astype(F32)
+    def drafter(i, buf):
+        buf[...] = jnp.dot(sc_ref[...].reshape(rows, depth), u_ref[:, columns(i)], preferred_element_type=F32)
+
+    def gather_stats(i, buf):
+        for b in range(rows // 32):
+            at = slice(b * 32, (b + 1) * 32)
+            logits = buf[at, :].astype(BF16)
+            for h in range(2):
+                g_ref[pl.ds(home(2 * b + h), 16), columns(i)] = logits[h * 16:(h + 1) * 16]
+            piece = logits.astype(F32)
             tiles = [piece[:, j * LANES:(j + 1) * LANES] for j in range(CHUNK // LANES)]
             old = m_ref[at, :]
             top = old
@@ -200,25 +236,16 @@
             m_ref[at, :] = top
             z_ref[at, :] = total
 
-    @pl.loop(0, chunks)
-    def _(i):
-        u_copy(i).wait()
-        drafter(i, 0, 3)
-        log_sum_rows(v_ref, jnp.minimum(i, rows // 32 - 1), lse_ref)
-
-    pack_rows(lse_ref, vst_ref, rows)
-
-    @pl.loop(1, n_t)
-    def _(k):
-        pltpu.make_async_remote_copy(
-            vst_ref.at[0], vst_ref.at[k], vs_send, vs_recv,
-            device_id=(dp, lax.rem(t + k, n_t)), device_id_type=MESH).start()
-
-    wait_bytes(sc_ref.at[3], r3_sem)
-
-    @pl.loop(0, chunks)
-    def _(i):
-        drafter(i, 3, 4)
+    drafter(0, even_ref)
+
+    @pl.loop(0, chunks // 2)
+    def _(j):
+        drafter(2 * j + 1, odd_ref)
+        gather_stats(2 * j, even_ref)
+        drafter(2 * j + 2, even_ref)
+        gather_stats(2 * j + 1, odd_ref)
+
+    gather_stats(chunks - 1, even_ref)
 
     for b in range(rows // 16):
         at = slice(b * 16, (b + 1) * 16)
@@ -336,7 +363,7 @@
     def add_hop(i, side):
         k, col = (3, left(i)) if side == 0 else (1, right(i))
         p_ref[slab(k), col] = (p_ref[slab(k), col].astype(F32) + f_ref[:, col].astype(F32)).astype(BF16)
-        y_copy(k, col, s_ref, s_recv.at[i, side], down if side == 0 else up).start()
+        y_copy(k, col, out_s, s_recv, down if side == 0 else up).start()
 
     @pl.loop(0, chunks)
     def _(i):
@@ -344,6 +371,16 @@
         add_hop(i, 0)
         y_copy(2, right(i), f_ref, f_recv.at[i, 1], up).wait_recv()
         add_hop(i, 1)
+
+    wait_bytes(o_ref, o_recv)
+
+    @pl.loop(0, chunks)
+    def _(i):
+        cols = columns(i)
+        p_ref[slab(0), cols] = (p_ref[slab(0), cols].astype(F32) + o_ref[:, cols].astype(F32)).astype(BF16)
+
+    a_copy = pltpu.make_async_copy(p_ref.at[slab(0)], out_a, a_sem)
+    a_copy.start()
 
     wait_bytes(gr_ref.at[pl.ds(0, n_t - 1)], n_recv)
     own = pl.ds(pl.multiple_of(t * owned, owned), owned)
@@ -357,16 +394,8 @@
     inner = jnp.mean(grad * normed, axis=-1, keepdims=True)
     out_h[...] = (inverse * (grad - normed * inner)).astype(BF16)
 
-    wait_bytes(o_ref, o_recv)
-
-    @pl.loop(0, chunks)
-    def _(i):
-        y_copy(3, left(i), s_ref, s_recv.at[i, 0], down).wait_recv()
-        y_copy(1, right(i), s_ref, s_recv.at[i, 1], up).wait_recv()
-        cols = columns(i)
-        out_u[:, cols] = (
-            p_ref[slab(0), cols].astype(F32) + o_ref[:, cols].astype(F32) + s_ref[:, cols].astype(F32)).astype(BF16)
-
+    a_copy.wait()
+    wait_bytes(out_s, s_recv)
     for part_sent in (sc_ref.at[0], sc_ref.at[0], sc_ref.at[3], sc_ref.at[0, 0, pl.ds(0, 3)], sc_ref.at[0, 0, pl.ds(0, 3)]):
         wait_bytes(part_sent, ag_send)
     wait_bytes(vst_ref.at[pl.ds(0, n_t - 1)], vs_send)
@@ -377,6 +406,11 @@
     wait_bytes(gr_ref.at[pl.ds(0, n_t - 1)], n_send)
 
 
+def finish(own_ref, sent_ref, hid_ref, out_u, out_h):
+    out_u[...] = (own_ref[...].astype(F32) + sent_ref[...].astype(F32)).astype(BF16)
+    out_h[...] = hid_ref[...]
+
+
 def body(n_dp, n_t, hidden, norm_gain, unembed, verifier_logits, served_ids, accepted):
     owned, depth = hidden.shape
     rows, width = verifier_logits.shape
@@ -385,15 +419,18 @@
     vmem = pl.BlockSpec(memory_space=pltpu.VMEM)
     hbm = pl.BlockSpec(memory_space=pl.ANY)
     dma = pltpu.SemaphoreType.DMA
-    return pl.pallas_call(
+    own, sent, grad_hidden = pl.pallas_call(
         functools.partial(kernel, n_dp, n_t),
         out_shape=(
+            jax.ShapeDtypeStruct((part, width), BF16),
             jax.ShapeDtypeStruct((part, width), BF16),
             jax.ShapeDtypeStruct((owned, depth), BF16),
         ),
         in_specs=[vmem, vmem, hbm, hbm, vmem, vmem],
-        out_specs=(vmem, vmem),
+        out_specs=(hbm, hbm, vmem),
         scratch_shapes=[
+            pltpu.VMEM((rows, CHUNK), F32),
+            pltpu.VMEM((rows, CHUNK), F32),
             pltpu.VMEM((depth, width), BF16),
             pltpu.VMEM((rows, width), BF16),
             pltpu.VMEM((rows, width), BF16),
@@ -405,7 +442,6 @@
             pltpu.VMEM((depth // 2, width), BF16),
             pltpu.VMEM((part, width), BF16),
             pltpu.VMEM((part, width), BF16),
-            pltpu.VMEM((part, width), BF16),
             pltpu.VMEM((rows, depth), BF16),
             pltpu.VMEM((n_t, owned, depth), BF16),
             pltpu.VMEM((rows, LANES), F32),
@@ -418,8 +454,8 @@
             pltpu.VMEM((rows, LANES), F32),
             pltpu.VMEM((n_t, 8, LANES), F32),
             pltpu.VMEM((n_t, 8, LANES), F32),
-            dma, dma((chunks,)), dma, dma((2, SIDE)), dma((2, SIDE, 2)), dma, dma, dma, dma, dma, dma, dma,
-            dma, dma((chunks,)), dma, dma((chunks, 2)), dma, dma((chunks, 2)), dma, dma,
+            dma, dma((chunks,)), dma, dma((WAVES, 2, SIDE)), dma((WAVES, 2, SIDE, 2)), dma((WAVES,)), dma, dma, dma, dma, dma, dma,
+            dma, dma((chunks,)), dma, dma((chunks, 2)), dma, dma, dma, dma, dma,
         ],
         compiler_params=pltpu.CompilerParams(
             collective_id=0, has_side_effects=True, vmem_limit_bytes=62 * 1024 * 1024),
@@ -427,6 +463,20 @@
             flops=6 * rows * depth * width, bytes_accessed=2 * (depth + rows + part) * width,
             transcendentals=4 * rows * width),
     )(hidden, norm_gain, unembed, verifier_logits, served_ids.reshape(rows // LANES, LANES), accepted.reshape(1, rows // DRAFT))
+    steps = 4
+    block = pl.BlockSpec((part // steps, width), lambda i: (i, 0))
+    small = pl.BlockSpec((owned, depth), lambda i: (0, 0))
+    return pl.pallas_call(
+        finish,
+        grid=(steps,),
+        out_shape=(
+            jax.ShapeDtypeStruct((part, width), BF16),
+            jax.ShapeDtypeStruct((owned, depth), BF16),
+        ),
+        in_specs=[block, block, small],
+        out_specs=(block, small),
+        compiler_params=pltpu.CompilerParams(vmem_limit_bytes=62 * 1024 * 1024),
+    )(own, sent, grad_hidden)
 
 
 def solution(mesh):

time: 112 us -> 110 us (0.982)
  local copies, waits for them, and re-layouts: 4.41 us -> 0 us
  Pallas kernels: 107 us -> 109 us
    unnamed x2 -> x0, local copies, waits for them, and re-layouts: 4.41 us -> none
    pallas_call x0 -> x1, Pallas kernels: none -> 4.18 us  [body(): pl.pallas_call(finish, grid=(steps,), out_shape=(jax.ShapeDtypeStruct((pa...]
    pallas_call x1, Pallas kernels: 107 us -> 105 us  [body(): pl.pallas_call(functools.partial(kernel, n_dp, n_t), out_shape=(jax.Shape...]
where the time goes in v3:
time: 110 us
  Pallas kernels  109 us (99%)
    pallas_call x1, Pallas kernels, body(): pl.pallas_call(functools.partial(kernel, n_dp, n_t), out_shape=(jax.Shape...  105 us
    pallas_call x1, Pallas kernels, body(): pl.pallas_call(finish, grid=(steps,), out_shape=(jax.ShapeDtypeStruct((pa...  4.18 us

profile of v3, /device:TPU:1, one launch (start us, length us, event | category | flops | bytes accessed | tf_op | source)
XLA Modules:
  0.0 109.7 jit_solution(10264373526265600711)
XLA Ops:
  0.6 104.8 %shard_map.77 = (bf16[192,4864]{1,0:T(8,128)(2,1)}, bf16[192,4864]{1,0:T(8,128)(2,1)}, bf16[32,1536]{1,0:T(8,128)(2,1)}) custom-call(bf16[32,1536]{1,0:T(8,128)(2,1)} %hid_ref.1, f32[1536]{0:T(1024)} %gain_ref.1, bf16[1536,4864]{1,0:T(8,128)(2,1)} %u_hbm.1, bf16[512,4864]{1,0:T(8,128)(2,1)} %v_hbm.1, s32[4,128]{1,0:T(4,128)} %bitcast.2, s32[1,64]{1,0:T(1,128)} %bitcast.3), custom_call_target="tpu_custom_call" | custom-call | flops 22951231488 | bytes 21790720 | tf_op jit(solution)/shard_map/pallas_call | solution.py:422
  105.5 4.2 %shard_map.78 = (bf16[192,4864]{1,0:T(8,128)(2,1)}, bf16[32,1536]{1,0:T(8,128)(2,1)}) custom-call(bf16[192,4864]{1,0:T(8,128)(2,1)} %get-tuple-element.5.own_ref, bf16[192,4864]{1,0:T(8,128)(2,1)} %get-tuple-element.6.sent_ref, bf16[32,1536]{1,0:T(8,128)(2,1)} %get-tuple-element.7.hid_ref), custom_call_target="tpu_custom_call" | custom-call | tf_op jit(solution)/shard_map/pallas_call | solution.py:469

commit v4 on v3

--- a/solution.py
+++ b/solution.py
@@ -10,6 +10,10 @@
 DRAFT = 8
 SIDE = 4
 WAVES = 1
+DIRECT = (2, 3)
+FAR_FIRST = sorted(
+    ((dz, dx) for dz in range(SIDE) for dx in range(SIDE) if dz or dx),
+    key=lambda d: -sum(min(c, SIDE - c) for c in d))
 LOG_LOW = -1.6094379124341003
 MESH = pl.DeviceIdType.MESH
 F32 = jnp.float32
@@ -70,6 +74,17 @@
     up = (lax.rem(dp + 2, n_dp), t)
     down = (lax.rem(dp + n_dp - 2, n_dp), t)
 
+    z, x = t // SIDE, lax.rem(t, SIDE)
+
+    def peer(dz, dx):
+        return (dp, lax.rem(z + dz, SIDE) * SIDE + lax.rem(x + dx, SIDE))
+
+    barrier = pltpu.get_barrier_semaphore()
+    for dz, dx in FAR_FIRST:
+        pl.semaphore_signal(barrier, inc=1, device_id=peer(dz, dx), device_id_type=MESH)
+    for other in (partner, up, down):
+        pl.semaphore_signal(barrier, inc=1, device_id=other, device_id_type=MESH)
+
     v_copy = pltpu.make_async_copy(v_hbm, v_ref, v_sem)
     v_copy.start()
 
@@ -83,16 +98,6 @@
     def _(i):
         u_copy(i).start()
 
-    barrier = pltpu.get_barrier_semaphore()
-
-    @pl.loop(1, n_t)
-    def _(k):
-        pl.semaphore_signal(barrier, inc=1, device_id=(dp, lax.rem(t + k, n_t)), device_id_type=MESH)
-
-    for other in (partner, up, down):
-        pl.semaphore_signal(barrier, inc=1, device_id=other, device_id_type=MESH)
-
-    z, x = t // SIDE, lax.rem(t, SIDE)
     place = (x, z)
 
     def first_axis(half, off):
@@ -125,6 +130,12 @@
         return pltpu.make_async_remote_copy(
             sc_ref.at[1 if back else 2, half, o, :, cols], sc_ref.at[3, half, o, :, cols], ag_send, r3_sem.at[w],
             device_id=second_axis(half, SIDE - 1 if back else 1), device_id_type=MESH)
+
+    def far_copy(w, half, off):
+        o = lax.rem(place[half] + SIDE - off, SIDE)
+        return pltpu.make_async_remote_copy(
+            sc_ref.at[0, half, o], sc_ref.at[3, half, o], ag_send, r3_sem.at[w],
+            device_id=second_axis(half, 2), device_id_type=MESH)
 
     def begin(w):
         for off in (1, 3, 2):
@@ -137,6 +148,8 @@
     def forward_cross(w, off):
         for half in range(2):
             line_copy(w, half, off).wait_recv()
+            if off in DIRECT:
+                far_copy(w, half, off).start()
             for back in range(2):
                 cross_copy(w, half, off, back).start()
 
@@ -144,7 +157,8 @@
         for half in range(2):
             for back in range(2):
                 cross_copy(w, half, off, back).wait_recv()
-                relay_copy(w, half, off, back).start()
+                if off not in DIRECT:
+                    relay_copy(w, half, off, back).start()
 
     def gathered(w):
         wait_bytes(sc_ref.at[3, :, :, :, pl.ds(w * span, span)], r3_sem.at[w])
@@ -194,11 +208,10 @@
     verifier(13, rows // 32)
     pack_rows(lse_ref, vst_ref, rows)
 
-    @pl.loop(1, n_t)
-    def _(k):
+    for dz, dx in FAR_FIRST:
         pltpu.make_async_remote_copy(
-            vst_ref.at[0], vst_ref.at[k], vs_send, vs_recv,
-            device_id=(dp, lax.rem(t + k, n_t)), device_id_type=MESH).start()
+            vst_ref.at[0], vst_ref.at[dz * SIDE + dx], vs_send, vs_recv,
+            device_id=peer(dz, dx), device_id_type=MESH).start()
 
     gathered(0)
 
@@ -254,11 +267,10 @@
         lse_ref[pl.ds(home(b), 16), :] = jnp.broadcast_to(top + jnp.log(total), (16, LANES))
     pack_rows(lse_ref, dst_ref, rows)
 
-    @pl.loop(1, n_t)
-    def _(k):
+    for dz, dx in FAR_FIRST:
         pltpu.make_async_remote_copy(
-            dst_ref.at[0], dst_ref.at[k], ds_send, ds_recv,
-            device_id=(dp, lax.rem(t + k, n_t)), device_id_type=MESH).start()
+            dst_ref.at[0], dst_ref.at[dz * SIDE + dx], ds_send, ds_recv,
+            device_id=peer(dz, dx), device_id_type=MESH).start()
 
     for b in range(rows // 16):
         gn_ref[pl.ds(home(b), 16), :] = sc_ref[b // 8, b // 4 % 2, b % 4]

time: 110 us -> 109 us (level)
  no operation moved by 1% of the time
where the time goes in v4:
time: 109 us
  Pallas kernels  108 us (99%)
    pallas_call x1, Pallas kernels, body(): pl.pallas_call(functools.partial(kernel, n_dp, n_t), out_shape=(jax.Shape...  104 us
    pallas_call x1, Pallas kernels, body(): pl.pallas_call(finish, grid=(steps,), out_shape=(jax.ShapeDtypeStruct((pa...  4.18 us

profile of v4, /device:TPU:1, one launch (start us, length us, event | category | flops | bytes accessed | tf_op | source)
XLA Modules:
  0.0 108.9 jit_solution(7932192627985330336)
XLA Ops:
  0.6 104.1 %shard_map.77 = (bf16[192,4864]{1,0:T(8,128)(2,1)}, bf16[192,4864]{1,0:T(8,128)(2,1)}, bf16[32,1536]{1,0:T(8,128)(2,1)}) custom-call(bf16[32,1536]{1,0:T(8,128)(2,1)} %hid_ref.1, f32[1536]{0:T(1024)} %gain_ref.1, bf16[1536,4864]{1,0:T(8,128)(2,1)} %u_hbm.1, bf16[512,4864]{1,0:T(8,128)(2,1)} %v_hbm.1, s32[4,128]{1,0:T(4,128)} %bitcast.2, s32[1,64]{1,0:T(1,128)} %bitcast.3), custom_call_target="tpu_custom_call" | custom-call | flops 22951231488 | bytes 21790720 | tf_op jit(solution)/shard_map/pallas_call | solution.py:434
  104.8 4.2 %shard_map.78 = (bf16[192,4864]{1,0:T(8,128)(2,1)}, bf16[32,1536]{1,0:T(8,128)(2,1)}) custom-call(bf16[192,4864]{1,0:T(8,128)(2,1)} %get-tuple-element.5.own_ref, bf16[192,4864]{1,0:T(8,128)(2,1)} %get-tuple-element.6.sent_ref, bf16[32,1536]{1,0:T(8,128)(2,1)} %get-tuple-element.7.hid_ref), custom_call_target="tpu_custom_call" | custom-call | tf_op jit(solution)/shard_map/pallas_call | solution.py:481

commit v5 on v4

--- a/solution.py
+++ b/solution.py
@@ -337,27 +337,45 @@
             jnp.dot(ot_ref[...], g_ref[:, columns(i)], preferred_element_type=F32)
             + jnp.dot(pt_ref[...], gp_ref[:, columns(i)], preferred_element_type=F32)).astype(BF16)
 
-    def first_sends(i):
+    def far_sends(i):
         y_copy(2, left(i), f_ref, f_recv.at[i, 0], down).start()
         y_copy(2, right(i), f_ref, f_recv.at[i, 1], up).start()
+
+    def near_sends(i):
         y_copy(1, left(i), o_ref, o_recv, up).start()
         y_copy(3, right(i), o_ref, o_recv, down).start()
+
+    def product_of(k, i):
+        rows_of = slice(k * part, (k + 1) * part)
+        p_ref[rows_of, columns(i)] = (
+            jnp.dot(ot_ref[rows_of, :], g_ref[:, columns(i)], preferred_element_type=F32)
+            + jnp.dot(pt_ref[rows_of, :], gp_ref[:, columns(i)], preferred_element_type=F32)).astype(BF16)
 
     grads(0)
     g_copy(0).start()
     wait_bytes(pt_ref, pt_recv)
-
-    @pl.loop(1, chunks)
+    grads(1)
+    g_copy(1).start()
+    g_copy(0).wait_recv()
+    product_of(2, 0)
+    far_sends(0)
+    for k in (1, 3, 0):
+        product_of(k, 0)
+    near_sends(0)
+
+    @pl.loop(2, chunks)
     def _(i):
         grads(i)
         g_copy(i).start()
         g_copy(i - 1).wait_recv()
         product(i - 1)
-        first_sends(i - 1)
+        far_sends(i - 1)
+        near_sends(i - 1)
 
     g_copy(chunks - 1).wait_recv()
     product(chunks - 1)
-    first_sends(chunks - 1)
+    far_sends(chunks - 1)
+    near_sends(chunks - 1)
 
     @pl.loop(0, depth // CHUNK)
     def _(n):
@@ -475,7 +493,7 @@
             flops=6 * rows * depth * width, bytes_accessed=2 * (depth + rows + part) * width,
             transcendentals=4 * rows * width),
     )(hidden, norm_gain, unembed, verifier_logits, served_ids.reshape(rows // LANES, LANES), accepted.reshape(1, rows // DRAFT))
-    steps = 4
+    steps = 3
     block = pl.BlockSpec((part // steps, width), lambda i: (i, 0))
     small = pl.BlockSpec((owned, depth), lambda i: (0, 0))
     return pl.pallas_call(

time: 109 us -> 109 us (level)
  no operation moved by 1% of the time
where the time goes in v5:
time: 109 us
  Pallas kernels  108 us (99%)
    pallas_call x1, Pallas kernels, body(): pl.pallas_call(functools.partial(kernel, n_dp, n_t), out_shape=(jax.Shape...  104 us
    pallas_call x1, Pallas kernels, body(): pl.pallas_call(finish, grid=(steps,), out_shape=(jax.ShapeDtypeStruct((pa...  4.19 us

profile of v5, /device:TPU:1, one launch (start us, length us, event | category | flops | bytes accessed | tf_op | source)
XLA Modules:
  0.0 108.7 jit_solution(8258706756806378219)
XLA Ops:
  0.6 103.9 %shard_map.77 = (bf16[192,4864]{1,0:T(8,128)(2,1)}, bf16[192,4864]{1,0:T(8,128)(2,1)}, bf16[32,1536]{1,0:T(8,128)(2,1)}) custom-call(bf16[32,1536]{1,0:T(8,128)(2,1)} %hid_ref.1, f32[1536]{0:T(1024)} %gain_ref.1, bf16[1536,4864]{1,0:T(8,128)(2,1)} %u_hbm.1, bf16[512,4864]{1,0:T(8,128)(2,1)} %v_hbm.1, s32[4,128]{1,0:T(4,128)} %bitcast.2, s32[1,64]{1,0:T(1,128)} %bitcast.3), custom_call_target="tpu_custom_call" | custom-call | flops 22951231488 | bytes 21790720 | tf_op jit(solution)/shard_map/pallas_call | solution.py:452
  104.5 4.2 %shard_map.78 = (bf16[192,4864]{1,0:T(8,128)(2,1)}, bf16[32,1536]{1,0:T(8,128)(2,1)}) custom-call(bf16[192,4864]{1,0:T(8,128)(2,1)} %get-tuple-element.5.own_ref, bf16[192,4864]{1,0:T(8,128)(2,1)} %get-tuple-element.6.sent_ref, bf16[32,1536]{1,0:T(8,128)(2,1)} %get-tuple-element.7.hid_ref), custom_call_target="tpu_custom_call" | custom-call | tf_op jit(solution)/shard_map/pallas_call | solution.py:499
